TPU v7x, 128 devices: a whole 4x4x4 slice. The times are simulated.
128 devices in a mesh: row: 8 (over y, z_lo), col: 16 (over x, z_hi, core).
Axes of the slice: x: 4, y: 4, z: 4 (z_hi: 2, z_lo: 2; z = z_hi * 2 + z_lo), core: 2. Of those that a mesh axis runs over, the one named last changes fastest.
Arguments:
- tokens: float32 [16384, 2048], P(('row', 'col')), may hold values from -6 to 6
- cotangent: float32 [16384, 2048], P(('row', 'col'))
- doc_starts: int32 [4], replicated, may hold values from 0 to 16383, as said below
- mixer_w: float32 [4, 2048, 2048], P(None, 'row', 'col'), may hold values from -0.125 to 0.125
- ffn_w: float32 [3, 2048, 5632], P(None, 'row', 'col'), may hold values from -0.125 to 0.125
- gains: float32 [2, 2048], replicated, may hold values from 0.5 to 1.5
- taps: float32 [3, 2048], P(None, 'col'), may hold values from -3 to 3
- mixer_m: float32 [4, 2048, 2048], P(None, 'row', 'col'), may hold values from -160 to 160
- mixer_v: float32 [4, 2048, 2048], P(None, 'row', 'col'), may hold values from 3440.64 to 13762.56
- ffn_m: float32 [3, 2048, 5632], P(None, 'row', 'col'), may hold values from -128 to 128
- ffn_v: float32 [3, 2048, 5632], P(None, 'row', 'col'), may hold values from 2457.6 to 9830.4
- gain_m: float32 [2, 2048], replicated, may hold values from -320 to 320
- gain_v: float32 [2, 2048], replicated, may hold values from 13762.56 to 55705.6
- tap_m: float32 [3, 2048], P(None, 'col'), may hold values from -160 to 160
- tap_v: float32 [3, 2048], P(None, 'col'), may hold values from 3440.64 to 13762.56
Outputs:
- output: float32 [16384, 2048], P(('row', 'col'))
- input_grad: float32 [16384, 2048], P(('row', 'col'))
- mixer_grad: float32 [4, 2048, 2048], P(None, 'row', 'col')
- mixer_new: float32 [4, 2048, 2048], P(None, 'row', 'col')
- mixer_m_new: float32 [4, 2048, 2048], P(None, 'row', 'col')
- mixer_v_new: float32 [4, 2048, 2048], P(None, 'row', 'col')
- ffn_grad: float32 [3, 2048, 5632], P(None, 'row', 'col')
- ffn_new: float32 [3, 2048, 5632], P(None, 'row', 'col')
- ffn_m_new: float32 [3, 2048, 5632], P(None, 'row', 'col')
- ffn_v_new: float32 [3, 2048, 5632], P(None, 'row', 'col')
- gain_grad: float32 [2, 2048], replicated
- gain_new: float32 [2, 2048], replicated
- gain_m_new: float32 [2, 2048], replicated
- gain_v_new: float32 [2, 2048], replicated
- tap_grad: float32 [3, 2048], P(None, 'col')
- tap_new: float32 [3, 2048], P(None, 'col')
- tap_m_new: float32 [3, 2048], P(None, 'col')
- tap_v_new: float32 [3, 2048], P(None, 'col')
Inputs may be any that keep to these rules, and one draw needn't show every extreme that they name: `doc_starts`: the first entry is 0, the last is 16383, and the entries strictly increase; document 1 begins within the first 2048 tokens and ends within the last 2048 tokens.
All inputs are finite; a program needn't handle non-finite values.
Results may differ from a plain program's by a relative error of at most 0.025.
Values may be sent and summed in bfloat16 or wider, within the bound.
A program may use at most 192 MiB of HBM per device.

v0:
```python
import jax
import jax.numpy as jnp
from jax import lax
from jax.sharding import PartitionSpec as P

STEP = 5


NORM_EPS = 1e-05
BETA_ONE = 0.9
BETA_TWO = 0.95
ADAM_EPS = 1e-08
MATRIX_DECAY = 0.1
MATRIX_RATE = 0.03
SMALL_RATE = 0.3


def from_behind(array, axis, by):
    length = lax.axis_size(axis)
    pairs = [(i, i + by) for i in range(length) if 0 <= i + by < length]
    return lax.ppermute(array, axis, pairs)


def trans_dot(left, right):
    return lax.dot_general(
        left, right, (((1,), (1,)), ((), ())), preferred_element_type=jnp.float32
    )


def rows_dot(left, right):
    return lax.dot_general(
        left, right, (((0,), (0,)), ((), ())), preferred_element_type=jnp.float32
    )


def norm_scale(values):
    return lax.rsqrt(jnp.mean(values * values, axis=1, keepdims=True) + NORM_EPS)


def norm_backward(incoming, normalized, scale, gain):
    scaled = incoming * gain
    return scale * (scaled - normalized * jnp.mean(scaled * normalized, axis=1, keepdims=True))


def adam_update(weight, gradient, first, second, step_rate, decay_rate):
    first_new = BETA_ONE * first + (1.0 - BETA_ONE) * gradient
    second_new = BETA_TWO * second + (1.0 - BETA_TWO) * gradient * gradient
    first_hat = first_new / (1.0 - BETA_ONE**STEP)
    second_hat = second_new / (1.0 - BETA_TWO**STEP)
    weight_new = weight - step_rate * (
        first_hat / (jnp.sqrt(second_hat) + ADAM_EPS) + decay_rate * weight
    )
    return (weight_new, first_new, second_new)


def body(
    tokens,
    cotangent,
    doc_starts,
    mixer_w,
    ffn_w,
    gains,
    taps,
    mixer_m,
    mixer_v,
    ffn_m,
    ffn_v,
    gain_m,
    gain_v,
    tap_m,
    tap_v,
):
    local_tokens = tokens.shape[0]
    model_width = tokens.shape[1]
    channels = taps.shape[1]
    row_tokens = local_tokens * lax.axis_size("col")
    column_start = lax.axis_index("col") * channels
    row_base = lax.axis_index("row") * row_tokens
    mixer_all, ffn_all = (
        lax.all_gather(mixer_w.astype(jnp.bfloat16), "row", axis=1, tiled=True),
        lax.all_gather(ffn_w.astype(jnp.bfloat16), "row", axis=1, tiled=True),
    )
    scale_one = norm_scale(tokens)
    normal_one = tokens * scale_one
    normed = (normal_one * gains[0]).astype(jnp.bfloat16)
    normed_all = lax.all_gather(normed, "col", axis=0, tiled=True)
    projected = jnp.einsum(
        "td,kdc->ktc", normed_all, mixer_all[:3], preferred_element_type=jnp.float32
    )
    input_gate = projected[0]
    output_gate = projected[1]
    conv_input = projected[2]
    mixed_bx = input_gate * conv_input
    prev_rows = from_behind(mixed_bx[row_tokens - 2 :], "row", 1)
    extended = jnp.concatenate([prev_rows, mixed_bx], axis=0)
    places = row_base - 2 + jnp.arange(row_tokens + 4, dtype=jnp.int32)
    start_flags = jnp.any(places[:, None] == doc_starts[None, :], axis=1)
    keep_all = jnp.where(start_flags, 0.0, 1.0).astype(jnp.float32)[:, None]
    pair_all = keep_all[1:] * keep_all[:-1]
    lag_one = keep_all[2 : 2 + row_tokens] * extended[1 : 1 + row_tokens]
    lag_two = pair_all[1 : 1 + row_tokens] * extended[:row_tokens]
    convolved = taps[2] * mixed_bx + taps[1] * lag_one + taps[0] * lag_two
    gated_out = (output_gate * convolved).astype(jnp.bfloat16)
    partial_out = trans_dot(gated_out, mixer_all[3])
    residual = tokens + lax.psum_scatter(partial_out, "col", scatter_dimension=0, tiled=True)
    scale_two = norm_scale(residual)
    ffn_in = (residual * scale_two * gains[1]).astype(jnp.bfloat16)
    ffn_in_all = lax.all_gather(ffn_in, "col", axis=0, tiled=True)
    normal_two = residual * scale_two
    gate_up = jnp.einsum("td,kdf->ktf", ffn_in_all, ffn_all[:2], preferred_element_type=jnp.float32)
    gate_proj = gate_up[0]
    up_proj = gate_up[1]
    activated = jax.nn.silu(gate_proj)
    hidden = (activated * up_proj).astype(jnp.bfloat16)
    output = residual + lax.psum_scatter(
        trans_dot(hidden, ffn_all[2]).astype(jnp.bfloat16), "col", scatter_dimension=0, tiled=True
    ).astype(jnp.float32)
    cotangent_all = lax.all_gather(cotangent.astype(jnp.bfloat16), "col", axis=0, tiled=True)
    grad_hidden = jnp.dot(cotangent_all, ffn_all[2], preferred_element_type=jnp.float32)
    sigmoid_gate = jax.nn.sigmoid(gate_proj)
    grad_gate = grad_hidden * up_proj * sigmoid_gate * (1.0 + gate_proj * (1.0 - sigmoid_gate))
    grad_gate_up = jnp.stack([grad_gate, grad_hidden * activated]).astype(jnp.bfloat16)
    ffn_part = jnp.concatenate(
        [
            jnp.einsum("td,ktf->kdf", ffn_in_all, grad_gate_up, preferred_element_type=jnp.float32),
            rows_dot(cotangent_all, hidden)[None],
        ],
        axis=0,
    )
    grad_ffn_part = jnp.einsum(
        "ktf,kdf->td", grad_gate_up, ffn_all[:2], preferred_element_type=jnp.float32
    )
    grad_ffn_in = lax.psum_scatter(grad_ffn_part, "col", scatter_dimension=0, tiled=True)
    gain_two_part = jnp.sum(grad_ffn_in * normal_two, axis=0)
    grad_residual = cotangent + norm_backward(grad_ffn_in, normal_two, scale_two, gains[1])
    residual_grad_all = lax.all_gather(
        grad_residual.astype(jnp.bfloat16), "col", axis=0, tiled=True
    )
    grad_gated = jnp.dot(residual_grad_all, mixer_all[3], preferred_element_type=jnp.float32)
    output_part = rows_dot(residual_grad_all, gated_out)
    grad_conv = grad_gated * output_gate
    grad_output_gate = grad_gated * convolved
    next_rows = from_behind(grad_conv[:2], "row", -1)
    ahead_rows = jnp.concatenate([grad_conv, next_rows], axis=0)
    grad_mixed = (
        taps[2] * grad_conv
        + taps[1] * keep_all[3 : 3 + row_tokens] * ahead_rows[1 : 1 + row_tokens]
        + taps[0] * pair_all[3 : 3 + row_tokens] * ahead_rows[2 : 2 + row_tokens]
    )
    tap_part = jnp.stack(
        [
            jnp.sum(grad_conv * lag_two, axis=0),
            jnp.sum(grad_conv * lag_one, axis=0),
            jnp.sum(grad_conv * mixed_bx, axis=0),
        ]
    )
    grad_proj = jnp.stack(
        [grad_mixed * conv_input, grad_output_gate, grad_mixed * input_gate]
    ).astype(jnp.bfloat16)
    input_part = jnp.einsum(
        "td,ktc->kdc", normed_all, grad_proj, preferred_element_type=jnp.float32
    )
    grad_normed_part = jnp.einsum(
        "ktc,kdc->td", grad_proj, mixer_all[:3], preferred_element_type=jnp.float32
    )
    grad_normed = lax.psum_scatter(
        grad_normed_part.astype(jnp.bfloat16), "col", scatter_dimension=0, tiled=True
    ).astype(jnp.float32)
    gain_one_part = jnp.sum(grad_normed * normal_one, axis=0)
    input_grad = grad_residual + norm_backward(grad_normed, normal_one, scale_one, gains[0])
    mixer_part = jnp.concatenate([input_part, output_part[None]], axis=0)
    mixer_grad, ffn_grad = (
        lax.psum_scatter(
            mixer_part.astype(jnp.bfloat16), "row", scatter_dimension=1, tiled=True
        ).astype(jnp.float32),
        lax.psum_scatter(
            ffn_part.astype(jnp.bfloat16), "row", scatter_dimension=1, tiled=True
        ).astype(jnp.float32),
    )
    tap_placed = lax.dynamic_update_slice(
        jnp.zeros((3, model_width), jnp.float32), tap_part, (0, column_start)
    )
    gain_grad, tap_total = lax.psum(
        (jnp.stack([gain_one_part, gain_two_part]), tap_placed), ("row", "col")
    )
    tap_grad = lax.dynamic_slice_in_dim(tap_total, column_start, channels, 1)
    mixer_new, mixer_m_new, mixer_v_new = adam_update(
        mixer_w, mixer_grad, mixer_m, mixer_v, MATRIX_RATE, MATRIX_DECAY
    )
    ffn_new, ffn_m_new, ffn_v_new = adam_update(
        ffn_w, ffn_grad, ffn_m, ffn_v, MATRIX_RATE, MATRIX_DECAY
    )
    gain_new, gain_m_new, gain_v_new = adam_update(
        gains, gain_grad, gain_m, gain_v, SMALL_RATE, 0.0
    )
    tap_new, tap_m_new, tap_v_new = adam_update(taps, tap_grad, tap_m, tap_v, SMALL_RATE, 0.0)
    return (
        output,
        input_grad,
        mixer_grad,
        mixer_new,
        mixer_m_new,
        mixer_v_new,
        ffn_grad,
        ffn_new,
        ffn_m_new,
        ffn_v_new,
        gain_grad,
        gain_new,
        gain_m_new,
        gain_v_new,
        tap_grad,
        tap_new,
        tap_m_new,
        tap_v_new,
    )


def solution(mesh):
    placed = (
        P(("row", "col"), None),
        P(("row", "col"), None),
        P(),
        P(None, "row", "col"),
        P(None, "row", "col"),
        P(),
        P(None, "col"),
        P(None, "row", "col"),
        P(None, "row", "col"),
        P(None, "row", "col"),
        P(None, "row", "col"),
        P(),
        P(),
        P(None, "col"),
        P(None, "col"),
    )
    return jax.shard_map(
        body,
        mesh=mesh,
        in_specs=placed,
        out_specs=(
            P(("row", "col"), None),
            P(("row", "col"), None),
            P(None, "row", "col"),
            P(None, "row", "col"),
            P(None, "row", "col"),
            P(None, "row", "col"),
            P(None, "row", "col"),
            P(None, "row", "col"),
            P(None, "row", "col"),
            P(None, "row", "col"),
            P(),
            P(),
            P(),
            P(),
            P(None, "col"),
            P(None, "col"),
            P(None, "col"),
            P(None, "col"),
        ),
        check_vma=False,
    )
```

profile of v0, /device:TPU:1, one launch (start us, length us, event | category | flops | bytes accessed | tf_op | source)
XLA Modules:
  0.0 1233.6 jit_solution(7444458683475526925)
XLA Ops:
  11.3 2.2 multiply_convert_fusion.8
  13.9 48.9 %all-gather.9.cloned.1.call-done = bf16[4,2048,128]{2,1,0:T(8,128)(2,1)} async-done(((bf16[4,256,128]{2,1,0:T(8,128)(2,1)}), bf16[4,2048,128]{2,1,0:T(8,128)(2,1)}) %all-gather.9.cloned.1.call-update) | async-done | bytes 2097168 | tf_op jit(solution)/shard_map/all_gather | solution.py:80
  62.7 78.3 %all-gather.7.cloned.1.call-done = bf16[2048,2048]{1,0:T(8,128)(2,1)} async-done(((bf16[128,2048]{1,0:T(8,128)(2,1)}), bf16[2048,2048]{1,0:T(8,128)(2,1)}) %all-gather.7.cloned.1.call-update) | async-done | bytes 8388624 | tf_op jit(solution)/shard_map/all_gather | solution.py:86
  141.1 7.3 fusion.14
  148.6 2.3 collective-permute-start
  153.1 9.3 fusion.67
  164.6 145.2 %reduce-scatter.7.cloned.1.call-done = f32[128,2048]{1,0:T(8,128)} async-done(((f32[2048,2048]{1,0:T(8,128)}), f32[128,2048]{1,0:T(8,128)}) %reduce-scatter.7.cloned.1.call-update) | async-done | bytes 1048592 | tf_op jit(solution)/shard_map/reduce_scatter | solution.py:105
  315.0 87.4 %all-gather.13.cloned.1.call-done = bf16[3,2048,352]{1,2,0:T(8,128)(2,1)} async-done(((bf16[3,256,352]{1,2,0:T(8,128)(2,1)}), bf16[3,2048,352]{1,2,0:T(8,128)(2,1)}) %all-gather.13.cloned.1.call-update) | async-done | bytes 4325392 | tf_op jit(solution)/shard_map/all_gather | solution.py:81
  402.3 78.9 %all-gather.11.cloned.1.call-done = bf16[2048,2048]{1,0:T(8,128)(2,1)} async-done(((bf16[128,2048]{1,0:T(8,128)(2,1)}), bf16[2048,2048]{1,0:T(8,128)(2,1)}) %all-gather.11.cloned.1.call-update) | async-done | bytes 8388624 | tf_op jit(solution)/shard_map/all_gather | solution.py:108
  481.2 11.8 fusion.8
  493.0 61.7 %all-gather.15.cloned.1.call-done = bf16[2048,2048]{1,0:T(8,128)(2,1)} async-done(((bf16[128,2048]{1,0:T(8,128)(2,1)}), bf16[2048,2048]{1,0:T(8,128)(2,1)}) %all-gather.15.cloned.1.call-update) | async-done | bytes 8388624 | tf_op jit(solution)/shard_map/all_gather | solution.py:118
  554.8 9.5 fusion.41
  565.9 10.3 convolution_bitcast_fusion
  576.5 12.3 %convolution_convert_fusion = bf16[2048,2048]{1,0:T(8,128)(2,1)} fusion(f32[2,2048,352]{1,2,0:T(8,128)} %fusion.8, bf16[3,2048,352]{1,2,0:T(8,128)(2,1)} %all-gather.13.cloned.1.call-done), kind=kOutput, calls=%fused_computation.10 | convolution fusion | flops 2961309696 | bytes 15597568 | tf_op jit(solution)/shard_map/dot_general | solution.py:25
  588.9 131.7 %reduce-scatter.11.cloned.1.call-done = f32[128,2048]{1,0:T(8,128)} async-done(((f32[2048,2048]{1,0:T(8,128)}), f32[128,2048]{1,0:T(8,128)}) %reduce-scatter.11.cloned.1.call-update) | async-done | bytes 1048592 | tf_op jit(solution)/shard_map/reduce_scatter | solution.py:133
  722.2 102.5 %reduce-scatter.9.cloned.1.call-done = bf16[128,2048]{1,0:T(8,128)(2,1)} async-done(((bf16[2048,2048]{1,0:T(8,128)(2,1)}), bf16[128,2048]{1,0:T(8,128)(2,1)}) %reduce-scatter.9.cloned.1.call-update) | async-done | bytes 524304 | tf_op jit(solution)/shard_map/reduce_scatter | solution.py:115
  824.7 3.5 fusion.82
  828.3 8.5 fusion.34
  836.8 8.9 fusion.17
  845.7 2.4 pad_maximum_fusion
  848.4 53.0 %all-gather.17.cloned.1.call-done = bf16[2048,2048]{1,0:T(8,128)(2,1)} async-done(((bf16[128,2048]{1,0:T(8,128)(2,1)}), bf16[2048,2048]{1,0:T(8,128)(2,1)}) %all-gather.17.cloned.1.call-update) | async-done | bytes 8388624 | tf_op jit(solution)/shard_map/all_gather | solution.py:136
  901.4 6.0 fusion.66
  914.4 3.5 fusion.31
  919.7 8.2 bitcast_convert_fusion
  932.6 61.2 %reduce-scatter.17.cloned.1.call-done = bf16[3,256,352]{1,2,0:T(8,128)(2,1)} async-done(((bf16[3,2048,352]{1,2,0:T(8,128)(2,1)}), bf16[3,256,352]{1,2,0:T(8,128)(2,1)}) %reduce-scatter.17.cloned.1.call-update) | async-done | bytes 540688 | tf_op jit(solution)/shard_map/reduce_scatter | solution.py:176
  993.8 4.0 multiply_subtract_fusion
  997.8 49.8 %reduce-scatter.15.cloned.1.call-done = bf16[4,256,128]{1,2,0:T(8,128)(2,1)} async-done(((bf16[4,2048,128]{1,2,0:T(8,128)(2,1)}), bf16[4,256,128]{1,2,0:T(8,128)(2,1)}) %reduce-scatter.15.cloned.1.call-update) | async-done | bytes 262160 | tf_op jit(solution)/shard_map/reduce_scatter | solution.py:173
  1047.6 2.4 multiply_subtract_fusion.1
  1050.0 2.1 copy.50
  1055.1 100.4 %reduce-scatter.13.cloned.1.call-done = bf16[128,2048]{1,0:T(8,128)(2,1)} async-done(((bf16[2048,2048]{1,0:T(8,128)(2,1)}), bf16[128,2048]{1,0:T(8,128)(2,1)}) %reduce-scatter.13.cloned.1.call-update) | async-done | bytes 524304 | tf_op jit(solution)/shard_map/reduce_scatter | solution.py:166
  1156.9 65.9 %all-reduce = (f32[2,2048]{1,0:T(2,128)S(1)}, f32[3,2048]{1,0:T(4,128)S(1)}) all-reduce(f32[2,2048]{1,0:T(2,128)S(1)} %pad_maximum_fusion.10, f32[3,2048]{1,0:T(4,128)S(1)} %maximum_dynamic-update-slice_fusion), channel_id=1, replica_groups=mesh['row'=8,'col'=16] {'row','col'}, use_global_device_ids=true, to_apply=%region_13.14 | all-reduce | flops 10240 | bytes 81920 | tf_op jit(solution)/shard_map/psum | solution.py:183
  1224.1 2.3 fusion.56
  (125 shorter events, 36.8 us)
Async XLA Ops:
  7.2 6.4 copy-start.20
  7.2 55.5 %all-gather.9.cloned.1.call-start = ((), (), s32[]{:S(2)}) async-start(), calls=%async_computation.7 | async-start | bytes 2359296 | tf_op jit(solution)/shard_map/all_gather | solution.py:80
  9.1 132.0 %all-gather.7.cloned.1.call-start = ((), (), s32[]{:S(2)}) async-start(), calls=%async_computation.6 | async-start | bytes 8912896 | tf_op jit(solution)/shard_map/all_gather | solution.py:86
  13.5 296.3 %reduce-scatter.7.cloned.1.call-start = ((), (), s32[]{:S(2)}) async-start(), calls=%async_computation.8 | async-start | bytes 17825792 | tf_op jit(solution)/shard_map/reduce_scatter | solution.py:105
  148.6 3.0 collective-permute-start
  153.1 9.3 copy-start.7
  162.5 147.3 %copy-start = (f32[128,2048]{1,0:T(8,128)S(1)}, f32[128,2048]{1,0:T(8,128)}, u32[]{:S(2)}) copy-start(f32[128,2048]{1,0:T(8,128)} %param.15) | copy-start | bytes 3145732
  162.5 239.8 %all-gather.13.cloned.1.call-start = ((), (), s32[]{:S(2)}) async-start(), calls=%async_computation.10 | async-start | bytes 4866048 | tf_op jit(solution)/shard_map/all_gather | solution.py:81
  164.6 316.7 %all-gather.11.cloned.1.call-start = ((), (), s32[]{:S(2)}) async-start(), calls=%async_computation.9 | async-start | bytes 8912896 | tf_op jit(solution)/shard_map/all_gather | solution.py:108
  312.2 242.6 %all-gather.15.cloned.1.call-start = ((), (), s32[]{:S(2)}) async-start(), calls=%async_computation.12 | async-start | bytes 8912896 | tf_op jit(solution)/shard_map/all_gather | solution.py:118
  314.4 406.3 %reduce-scatter.11.cloned.1.call-start = ((), (), s32[]{:S(2)}) async-start(), calls=%async_computation.13 | async-start | bytes 17825792 | tf_op jit(solution)/shard_map/reduce_scatter | solution.py:133
  554.8 11.1 copy-start.22
  576.3 248.4 %reduce-scatter.9.cloned.1.call-start = ((), (), s32[]{:S(2)}) async-start(), calls=%async_computation.11 | async-start | bytes 8912896 | tf_op jit(solution)/shard_map/reduce_scatter | solution.py:115
  588.9 312.6 %all-gather.17.cloned.1.call-start = ((), (), s32[]{:S(2)}) async-start(), calls=%async_computation.14 | async-start | bytes 8912896 | tf_op jit(solution)/shard_map/all_gather | solution.py:136
  828.2 165.6 %reduce-scatter.17.cloned.1.call-start = ((), (), s32[]{:S(2)}) async-start(), calls=%async_computation.17 | async-start | bytes 4866048 | tf_op jit(solution)/shard_map/reduce_scatter | solution.py:176
  828.3 8.5 copy-start.24
  828.3 8.5 copy-start.26
  848.2 59.2 %copy-start.5 = (f32[2048,128]{1,0:T(8,128)S(1)}, f32[2048,128]{1,0:T(8,128)}, u32[]{:S(2)}) copy-start(f32[2048,128]{1,0:T(8,128)} %get-tuple-element.85) | copy-start | bytes 3145732
  848.2 199.5 %reduce-scatter.15.cloned.1.call-start = ((), (), s32[]{:S(2)}) async-start(), calls=%async_computation.16 | async-start | bytes 2359296 | tf_op jit(solution)/shard_map/reduce_scatter | solution.py:173
  901.4 8.4 copy-start.21
  907.4 6.9 slice-start
  908.3 6.1 copy-start.11
  908.3 5.0 collective-permute-start.1
  919.4 236.1 %reduce-scatter.13.cloned.1.call-start = ((), (), s32[]{:S(2)}) async-start(), calls=%async_computation.15 | async-start | bytes 8912896 | tf_op jit(solution)/shard_map/reduce_scatter | solution.py:166
  929.0 64.8 %copy-start.4 = (f32[3,256,352]{1,2,0:T(8,128)S(1)}, f32[3,256,352]{1,2,0:T(8,128)}, u32[]{:S(2)}) copy-start(f32[3,256,352]{1,2,0:T(8,128)} %param.19) | copy-start | bytes 3244036
  1047.6 6.5 copy-start.10
  1050.0 172.8 %copy-start.18 = (f32[3,128]{1,0:T(4,128)S(1)}, f32[3,128]{1,0:T(4,128)}, u32[]{:S(2)}) copy-start(f32[3,128]{1,0:T(4,128)} %param.28) | copy-start | bytes 4612
  1050.0 172.8 %copy-start.19 = (f32[3,128]{1,0:T(4,128)S(1)}, f32[3,128]{1,0:T(4,128)}, u32[]{:S(2)}) copy-start(f32[3,128]{1,0:T(4,128)} %param.29) | copy-start | bytes 4612
  1050.0 173.4 %copy-start.13 = (f32[2,2048]{1,0:T(2,128)S(1)}, f32[2,2048]{1,0:T(2,128)}, u32[]{:S(2)}) copy-start(f32[2,2048]{1,0:T(2,128)} %param.20) | copy-start | bytes 49156
  1050.0 173.4 %copy-start.14 = (f32[2,2048]{1,0:T(2,128)S(1)}, f32[2,2048]{1,0:T(2,128)}, u32[]{:S(2)}) copy-start(f32[2,2048]{1,0:T(2,128)} %param.26) | copy-start | bytes 49156
  1050.0 173.4 %copy-start.15 = (f32[2,2048]{1,0:T(2,128)S(1)}, f32[2,2048]{1,0:T(2,128)}, u32[]{:S(2)}) copy-start(f32[2,2048]{1,0:T(2,128)} %param.27) | copy-start | bytes 49156
  1050.0 174.1 %copy-start.6 = (f32[128,2048]{1,0:T(8,128)S(1)}, f32[128,2048]{1,0:T(8,128)}, u32[]{:S(2)}) copy-start(f32[128,2048]{1,0:T(8,128)} %get-tuple-element.81) | copy-start | bytes 3145732
  (11 other events, 32.1 us)
Sparse Core Ops, SparseCore 0:
  10.3 52.4 all-gather.8
  65.7 75.3 all-gather.6
  162.6 147.1 reduce-scatter.6
  311.9 90.3 all-gather.12
  405.4 75.7 all-gather.10
  484.4 70.3 all-gather.14
  576.4 144.1 reduce-scatter.10
  725.0 99.6 reduce-scatter.8
  828.4 73.0 all-gather.16
  903.7 90.0 reduce-scatter.16
  996.4 51.2 reduce-scatter.14
  1052.4 102.9 reduce-scatter.12
where the time goes:
time: 1240 us; the launch traced here: 1230 us
  waiting for transfers between devices  1000 us (81%)
  matrix products  97 us (8%)
  blocking collectives  65.9 us (5%)
  other arithmetic  34.9 us (3%)
  between operations  14.9 us (1%)
  local copies, waits for them, and re-layouts  13.4 us (1%)
    reduce_scatter x1, waiting for transfers between devices, body(): lax.psum_scatter(partial_out, 'col', scatter_dimension=0, tiled=True)  145 us
    reduce_scatter x1, waiting for transfers between devices, body(): lax.psum_scatter(grad_ffn_part, 'col', scatter_dimension=0, tiled=True)  132 us
    reduce_scatter x1, waiting for transfers between devices, body(): lax.psum_scatter(trans_dot(hidden, ffn_all[2]).astype(jnp.bfloat16), 'col...  102 us
    reduce_scatter x1, waiting for transfers between devices, body(): lax.psum_scatter(grad_normed_part.astype(jnp.bfloat16), 'col', scatter_di...  100 us
    all_gather x1, waiting for transfers between devices, body(): lax.all_gather(ffn_w.astype(jnp.bfloat16), 'row', axis=1, tiled=True)  87.4 us
    all_gather x1, waiting for transfers between devices, body(): ffn_in_all = lax.all_gather(ffn_in, 'col', axis=0, tiled=True)  78.9 us
    all_gather x1, waiting for transfers between devices, body(): normed_all = lax.all_gather(normed, 'col', axis=0, tiled=True)  78.3 us
    psum x1, blocking collectives, body(): lax.psum((jnp.stack([gain_one_part, gain_two_part]), tap_placed), ('row',...  65.9 us
  transfers between devices with their start and end apart: 14, of which 14 were waited for; matrix products, arithmetic and copies ran while one was open for 8% of the time, Pallas kernels for 0%

commit v1 on v0

v1 whole, which is shorter than its diff:
```python
import jax
import jax.numpy as jnp
from jax import lax
from jax.experimental import pallas as pl
from jax.experimental.pallas import tpu as pltpu
from jax.sharding import PartitionSpec as P

STEP = 5


NORM_EPS = 1e-05
BETA_ONE = 0.9
BETA_TWO = 0.95
ADAM_EPS = 1e-08
MATRIX_DECAY = 0.1
MATRIX_RATE = 0.03
SMALL_RATE = 0.3

MESH = pl.DeviceIdType.MESH
BF16 = jnp.bfloat16
F32 = jnp.float32
RING = 4
PACE = "_sent"
ROWS = 8
LINK = 46.5e3
CORES = 280e3


def place():
    row, col = lax.axis_index("row"), lax.axis_index("col")
    return {"x": col // 4, "y": row // 2, "z": (col // 2) % 2 * 2 + row % 2, "k": col % 2}


def device_at(at):
    return (at["y"] * 2 + at["z"] % 2, at["x"] * 4 + at["z"] // 2 * 2 + at["k"])


def wrap(value, length=RING):
    return lax.rem(value + length, length)


class Work:
    def __init__(self, send_sems, recv_sems, local_sems):
        self.me = place()
        self.send_sems, self.recv_sems, self.local_sems = send_sems, recv_sems, local_sems
        self.sent, self.local = [], []
        self.count = self.local_count = 0
        self.now, self.free, self.due, self.flags, self.chains = 0.0, {}, {}, set(), []

    def near(self, axis, step):
        at = dict(self.me)
        at[axis] = wrap(at[axis] + step, 2 if axis == "k" else RING)
        return device_at(at)

    def target(self, way):
        axis, step = way
        if axis == "row":
            row, col = lax.axis_index("row"), lax.axis_index("col")
            return (wrap(row + step, ROWS), col + 2 - 4 * ((col // 2) % 2))
        return self.near(axis, step)

    def barrier(self, ways):
        sem = pltpu.get_barrier_semaphore()
        for axis, step in ways:
            pl.semaphore_signal(sem, inc=1, device_id=self.target((axis, -step)), device_id_type=MESH)
        pl.semaphore_wait(sem, len(ways))

    def send(self, source, target, way):
        copy = pltpu.make_async_remote_copy(
            src_ref=source,
            dst_ref=target,
            send_sem=self.send_sems.at[self.count],
            recv_sem=self.recv_sems.at[self.count],
            device_id=self.target(way),
            device_id_type=MESH,
        )
        copy.start()
        self.count += 1
        self.sent.append(copy)
        size = 1
        for extent in source.shape:
            size *= extent
        size *= jnp.dtype(source.dtype).itemsize
        begin = max(self.now, self.free.get(way, 0.0))
        self.free[way] = begin + size / (CORES if way[0] == "k" else LINK)
        self.due[id(copy)] = self.free[way] + (1.0 if way[0] == "k" else 2.0)
        return copy

    def copy(self, source, target, rate=1.4e6):
        copy = pltpu.make_async_copy(source, target, self.local_sems.at[self.local_count])
        copy.start()
        self.local_count += 1
        size = 1
        for extent in source.shape:
            size *= extent
        size *= jnp.dtype(source.dtype).itemsize
        begin = max(self.now, self.free.get("local", 0.0))
        self.free["local"] = begin + size / rate
        self.due[id(copy)] = self.free["local"] + 0.5
        self.local.append(copy)
        return copy

    def add(self, chain, rank=0):
        self.chains.append([next(chain), rank, len(self.chains), chain])

    def set(self, flag):
        self.flags.add(flag)

    def run(self):
        while self.chains:
            best, when = None, None
            for entry in self.chains:
                wish = entry[0]
                if isinstance(wish, str):
                    if wish not in self.flags:
                        continue
                    key = (0 if entry[1] == 0 else 1, entry[1], self.now, entry[2])
                elif isinstance(wish, float):
                    key = (0 if entry[1] == 0 else 1, entry[1], self.now, entry[2])
                else:
                    due = self.due[id(wish)]
                    if due <= self.now:
                        key = (0 if entry[1] == 0 else 1, entry[1], due, entry[2])
                    else:
                        key = (2, due, entry[1], entry[2])
                if best is None or key < when:
                    best, when = entry, key
            assert best is not None, self.flags
            wish = best[0]
            if not isinstance(wish, (str, float)):
                self.now = max(self.now, self.due[id(wish)]) + 0.05
                if any(wish is copy for copy in self.local):
                    wish.wait()
                    self.local = [copy for copy in self.local if copy is not wish]
                else:
                    wish.wait_recv()
            try:
                best[0] = next(best[3])
                if isinstance(best[0], float):
                    self.now += best[0]
            except StopIteration:
                self.chains = [entry for entry in self.chains if entry is not best]
        for copy in self.sent:
            copy.wait_send()
        for copy in self.local:
            copy.wait()


def gather_x(work, source, out, name, copy=False, hold=None):
    x, k = work.me["x"], work.me["k"]
    rows = source.shape[0]
    half = rows // 2
    low, high = pl.ds(0, half), pl.ds(half, half)
    right, left, other = ("x", 1), ("x", -1), ("k", 1)
    ahead, behind, across = wrap(x + 1), wrap(x - 1), wrap(x + 2)
    yield name + "_go"
    r0 = work.send(source.at[low], out.at[x, k, low], right)
    l1 = work.send(source.at[high], out.at[x, k, high], left)
    r1 = work.send(source.at[high], out.at[x, k, high], right)
    l0 = work.send(source.at[low], out.at[x, k, low], left)
    sib = [work.send(source, out.at[x, k], other)]
    if copy:
        work.copy(source, out.at[x, k])
    work.set(name + "_sent")

    def relay(at, part):
        sib.append(work.send(out.at[at, k, part], out.at[at, k, part], other))

    if hold is not None:
        yield hold
    yield r0
    far0 = work.send(out.at[behind, k, low], out.at[behind, k, low], right)
    relay(behind, low)
    yield l1
    far1 = work.send(out.at[ahead, k, high], out.at[ahead, k, high], left)
    relay(ahead, high)
    work.set(name + "_far")
    yield r1
    relay(behind, high)
    yield l0
    relay(ahead, low)
    yield far0
    relay(across, low)
    yield far1
    relay(across, high)
    for number, one in enumerate(sib):
        yield one
        if number == 0:
            work.set(name + "_own")
        if number == 4:
            work.set(name + "_near")
    work.set(name + "_all")


def add_into(target, first, second):
    rows = target.shape[-2]
    lead = target.shape[:-2]
    strip = 16

    def body(step, _):
        at = pl.ds(pl.multiple_of(step * strip, strip), strip)
        for m in range(lead[0] if lead else 1):
            here = (m, at) if lead else (at,)
            target[here] = (first[here].astype(F32) + second[here].astype(F32)).astype(BF16)
        return 0

    lax.fori_loop(0, rows // strip, body, 0)


def ring_places(x):
    return (wrap(x + 2), wrap(x + 1), wrap(x - 1), x)


def scatter_x(work, parts, box, hop, land, name):
    x, k = work.me["x"], work.me["k"]
    rows = box.shape[1]
    half = rows // 2
    low, high = pl.ds(0, half), pl.ds(half, half)
    right, left, other = ("x", 1), ("x", -1), ("k", 1)
    across, ahead, behind, own = ring_places(x)

    def swap():
        sib = {}
        for number, at in enumerate((across, ahead, behind, own)):
            yield name + str(number)
            sib[number] = work.send(parts.at[at, 1 - k], box.at[at], other)
            got.append(sib[number])
            work.set(name + "_swap" + str(number))

    got = []
    work.add(swap(), 0)
    yield name + "_swap0"
    yield got[0]
    add_into(box.at[across], parts.at[across, k], box.at[across])
    far0 = work.send(box.at[across, low], hop.at[0], right)
    far1 = work.send(box.at[across, high], hop.at[1], left)
    yield 0.3
    yield name + "_swap1"
    yield got[1]
    add_into(box.at[ahead], parts.at[ahead, k], box.at[ahead])
    r1 = work.send(box.at[ahead, high], land.at[0, high], right)
    yield 0.3
    yield name + "_swap2"
    yield got[2]
    add_into(box.at[behind], parts.at[behind, k], box.at[behind])
    l0 = work.send(box.at[behind, low], land.at[1, low], left)
    yield 0.3
    yield far0
    add_into(box.at[ahead, low], box.at[ahead, low], hop.at[0])
    r0 = work.send(box.at[ahead, low], land.at[0, low], right)
    yield 0.15
    yield far1
    add_into(box.at[behind, high], box.at[behind, high], hop.at[1])
    l1 = work.send(box.at[behind, high], land.at[1, high], left)
    work.set(name + "_sent")
    yield 0.15
    yield name + "_swap3"
    yield got[3]
    for copy in (r1, l0, r0, l1):
        yield copy
    work.set(name + "_done")


def block(ref, y, z, half, rows):
    column = pl.multiple_of((y * 2 + z % 2) * 256 + half * 128, 128)
    return ref.at[:, z // 2, rows, pl.ds(column, 128)]


def gather_yz(work, source, out, half, name):
    first, second = ("y", "z") if half == 0 else ("z", "y")
    rows = source.shape[1]
    cut = rows // 2
    low, high, whole = pl.ds(0, cut), pl.ds(cut, cut), pl.ds(0, rows)
    a, b = work.me[first], work.me[second]

    def slot(at_a, at_b, part):
        y, z = (at_a, at_b) if half == 0 else (at_b, at_a)
        return block(out, y, z, half, part)

    columns = pl.ds(half * 128, 128)
    up, down, forward, backward = (first, 1), (first, -1), (second, 1), (second, -1)
    a_behind, a_ahead, a_across = wrap(a - 1), wrap(a + 1), wrap(a + 2)
    b_behind, b_ahead = wrap(b - 1), wrap(b + 1)
    yield name + "_go" + str(half)
    mine = work.copy(source.at[:, :, columns], slot(a, b, whole))
    r0 = work.send(source.at[:, low, columns], slot(a, b, low), up)
    l1 = work.send(source.at[:, high, columns], slot(a, b, high), down)
    r1 = work.send(source.at[:, high, columns], slot(a, b, high), up)
    l0 = work.send(source.at[:, low, columns], slot(a, b, low), down)
    waits, last = [], []

    def spread(at, part, ref=None):
        ref = slot(at, b, part) if ref is None else ref
        waits.append(
            (
                at,
                part,
                work.send(ref, slot(at, b, part), forward),
                work.send(ref, slot(at, b, part), backward),
            )
        )

    def onward(number):
        at, part, plus, minus = waits[number]
        yield plus
        if part is low:
            last.append(work.send(slot(at, b_behind, part), slot(at, b_behind, part), forward))
        yield minus
        if part is high:
            last.append(work.send(slot(at, b_ahead, part), slot(at, b_ahead, part), backward))

    spread(a, low, source.at[:, low, columns])
    spread(a, high, source.at[:, high, columns])
    yield r0
    f0 = work.send(slot(a_behind, b, low), slot(a_behind, b, low), up)
    spread(a_behind, low)
    yield l1
    f1 = work.send(slot(a_ahead, b, high), slot(a_ahead, b, high), down)
    spread(a_ahead, high)
    yield from onward(0)
    yield r1
    spread(a_behind, high)
    yield l0
    spread(a_ahead, low)
    yield from onward(1)
    yield f0
    spread(a_across, low)
    yield f1
    spread(a_across, high)
    work.set(name + "_spread" + str(half))
    for number in range(2, 8):
        yield from onward(number)
        if number == 5:
            work.set(name + "_most" + str(half))
    work.set(name + "_sent" + str(half))
    for copy in last:
        yield copy
    yield mine
    work.set(name + "_all" + str(half))


def scatter_yz(work, parts, box, out, half, name):
    first, second = ("z", "y") if half == 0 else ("y", "z")
    rows = out.shape[1]
    cut = rows // 2
    low, high, whole = pl.ds(0, cut), pl.ds(cut, cut), pl.ds(0, rows)
    a, b = work.me[first], work.me[second]
    key = name + str(half)

    def slot(at_a, at_b, part):
        y, z = (at_b, at_a) if half == 0 else (at_a, at_b)
        return block(parts, y, z, half, part)

    across, ahead, behind, own = ring_places(a)
    up, down = (first, 1), (first, -1)

    def first_ring(number, at_b):
        base = 3 * number
        pick = lambda at, part: slot(at, at_b, part)
        yield name + "_go" + str(half)
        far0 = work.send(pick(across, low), box.at[base, :, low], up)
        far1 = work.send(pick(across, high), box.at[base, :, high], down)
        r1 = work.send(pick(ahead, high), box.at[base + 1, :, high], up)
        l0 = work.send(pick(behind, low), box.at[base + 2, :, low], down)
        yield far0
        add_into(pick(ahead, low), pick(ahead, low), box.at[base, :, low])
        r0 = work.send(pick(ahead, low), box.at[base + 1, :, low], up)
        yield far1
        add_into(pick(behind, high), pick(behind, high), box.at[base, :, high])
        l1 = work.send(pick(behind, high), box.at[base + 2, :, high], down)
        yield r1
        add_into(pick(own, high), pick(own, high), box.at[base + 1, :, high])
        yield l0
        add_into(pick(own, low), pick(own, low), box.at[base + 2, :, low])
        yield r0
        add_into(pick(own, low), pick(own, low), box.at[base + 1, :, low])
        yield l1
        add_into(pick(own, high), pick(own, high), box.at[base + 2, :, high])
        work.set(key + "_first" + str(number))

    places = ring_places(b)
    for number, at_b in enumerate(places):
        work.add(first_ring(number, at_b))
    b_across, b_ahead, b_behind, b_own = places
    forward, backward = (second, 1), (second, -1)
    yield key + "_first0"
    far0 = work.send(slot(a, b_across, low), box.at[12, :, low], forward)
    far1 = work.send(slot(a, b_across, high), box.at[12, :, high], backward)
    yield key + "_first1"
    r1 = work.send(slot(a, b_ahead, high), box.at[13, :, high], forward)
    yield far0
    add_into(slot(a, b_ahead, low), slot(a, b_ahead, low), box.at[12, :, low])
    r0 = work.send(slot(a, b_ahead, low), box.at[13, :, low], forward)
    yield key + "_first2"
    l0 = work.send(slot(a, b_behind, low), box.at[14, :, low], backward)
    yield far1
    add_into(slot(a, b_behind, high), slot(a, b_behind, high), box.at[12, :, high])
    l1 = work.send(slot(a, b_behind, high), box.at[14, :, high], backward)
    yield key + "_first3"
    mine = slot(a, b_own, whole)
    for copy in (r1, r0, l0, l1):
        yield copy
    for m in range(out.shape[0]):
        total = mine[m].astype(F32) + box[13, m].astype(F32) + box[14, m].astype(F32)
        out[m, :, half * 128 : (half + 1) * 128] = total.astype(out.dtype)
    work.set(key + "_done")


def sum_all(work, values, box, out, name):
    yield name + "_go"
    out[...] = values[...]
    me = work.me
    for turn, axis in enumerate(("z", "y", "x", "k")):
        length = 2 if axis == "k" else RING
        mine = box.at[turn, me[axis]]
        mine[...] = out[...]
        copies = [work.send(mine, mine, (axis, step)) for step in range(1, length)]
        for copy in copies:
            yield copy
        total = box[turn, 0]
        for number in range(1, length):
            total = total + box[turn, number]
        out[...] = total
    work.set(name + "_done")


ANY = pl.BlockSpec(memory_space=pl.ANY)
VMEM = pl.BlockSpec(memory_space=pltpu.VMEM)
SMEM = pl.BlockSpec(memory_space=pltpu.SMEM)
X_WAYS = (("x", 1), ("x", -1), ("k", 1))
YZ_WAYS = (("y", 1), ("y", -1), ("z", 1), ("z", -1))


def bf(*shape):
    return jax.ShapeDtypeStruct(shape, BF16)


def fl(*shape):
    return jax.ShapeDtypeStruct(shape, F32)


def call(name, number, body, args, outs, scratch, copies, local, ways, flops):
    def kernel(*refs):
        main, sems = refs[:-3], refs[-3:]
        work = Work(*sems)
        work.barrier(ways)
        body(work, *main)
        work.run()
        assert work.count <= copies and work.local_count <= local, (work.count, work.local_count)

    sems = [pltpu.SemaphoreType.DMA((copies,)), pltpu.SemaphoreType.DMA((copies,)), pltpu.SemaphoreType.DMA((local,))]
    return pl.pallas_call(
        kernel,
        out_shape=[shape for shape, _ in outs],
        in_specs=[spec for _, spec in args],
        out_specs=[spec for _, spec in outs],
        scratch_shapes=list(scratch) + sems,
        compiler_params=pltpu.CompilerParams(
            collective_id=number, has_side_effects=True, vmem_limit_bytes=60 << 20
        ),
        cost_estimate=pl.CostEstimate(flops=flops, bytes_accessed=40 << 20, transcendentals=0),
        name=name,
    )(*[array for array, _ in args])


def dot_nt(left, right):
    return lax.dot_general(left, right, (((1,), (1,)), ((), ())), preferred_element_type=F32)


def dot_tn(left, right):
    return lax.dot_general(left, right, (((0,), (0,)), ((), ())), preferred_element_type=F32)


def dot_nn(left, right):
    return lax.dot_general(left, right, (((1,), (0,)), ((), ())), preferred_element_type=F32)


def strips(rows, strip, body):
    def one(step, _):
        body(pl.ds(pl.multiple_of(step * strip, strip), strip))
        return 0

    lax.fori_loop(0, rows // strip, one, 0)


def keeps(starts, first, shape):
    places = first + lax.broadcasted_iota(jnp.int32, shape, 0)

    def keep(at):
        hit = at == starts[0]
        for number in range(1, 4):
            hit = jnp.logical_or(hit, at == starts[number])
        return jnp.where(hit, 0.0, 1.0).astype(F32)

    here = keep(places)
    return here, here * keep(places - 1)


def run_start(run, run_tokens):
    row, col = lax.axis_index("row"), lax.axis_index("col")
    return ((row * RING + run) * 2 + (col // 2) % 2) * run_tokens


SHARD, WIDTH = 128, 2048
RUN = 2 * SHARD
CH, HALF = 256, 128
HID = 352


def lags(ext, starts, run, at, lane):
    rows = 64
    lanes = slice(lane * HALF, (lane + 1) * HALF)
    one, two = keeps(starts, run_start(run, RUN) + at, (rows, HALF))
    mixed = ext[run, 8 + at : 8 + at + rows, lanes]
    return mixed, one * ext[run, 7 + at : 7 + at + rows, lanes], two * ext[run, 6 + at : 6 + at + rows, lanes]


def place_halo(ext, near, far):
    row, col = lax.axis_index("row"), lax.axis_index("col")
    late = (col // 2) % 2 == 1
    first = jnp.where(row > 0, far[...], 0.0)
    for run in range(RING):
        ext[run, 0:8] = jnp.where(late, near[run], first if run == 0 else near[run - 1])


def forward_mixer(tokens, cotangent, starts, mixer, ffn, gains, taps):
    def body(
        work, tokens, cotangent, starts, mixer, ffn, gains, taps,
        normed_out, cot_out, in_out, mix_out, ffn_out, proj_out, near_out, far_out, taps_out, residual, ffn_in_out,
        normed, weights, proj, ext, gated, parts, box, hop, land, cot, ffn_in,
    ):
        x, k = work.me["x"], work.me["k"]
        col = lax.axis_index("col")
        z_hi = (col // 2) % 2
        w_in, w_out = weights.at[0:3], weights.at[3:4]

        def opening():
            def norm(at):
                rows = tokens[at]
                scale = lax.rsqrt(jnp.mean(rows * rows, axis=1, keepdims=True) + NORM_EPS)
                normed[x, k, at] = (rows * scale * gains[0:1]).astype(BF16)

            strips(SHARD, 16, norm)
            work.set("normed_go")
            work.set("in_go0")
            work.set("in_go1")
            yield 1.0

            def cast(at):
                cot[at] = cotangent[at].astype(BF16)

            strips(SHARD, 16, cast)
            taps_out[z_hi] = taps[...]
            work.send(taps, taps_out.at[z_hi], ("z", 2))
            taps_copy.append(work.sent[-1])
            work.set("taps_sent")
            yield 0.5

        taps_copy = []

        def compute():
            yield "taps_sent"
            yield taps_copy[0]
            yield "normed_all"
            work.copy(normed, normed_out)
            yield "in_all0"
            yield "in_all1"
            tail = normed[:, 1, SHARD - 16 :].reshape(RING * 16, WIDTH)
            ends = dot_nt(tail, weights[0:3].reshape(3 * CH, WIDTH))
            mixed = (ends[:, :CH] * ends[:, 2 * CH :]).reshape(RING, 16, CH)
            ext[:, RUN - 8 : RUN + 8] = mixed
            sent = [
                work.send(ext.at[:, RUN : RUN + 8], near_out, ("z", 2)),
                work.send(ext.at[RING - 1, RUN : RUN + 8], far_out, ("row", 1)),
            ]
            yield 1.0

            def project(half, _):
                rows = normed[pl.ds(2 * half, 2)].reshape(2 * RUN, WIDTH)
                out = dot_nt(rows, weights[0:3].reshape(3 * CH, WIDTH))
                proj[pl.ds(2 * half, 2)] = out.reshape(2, RUN, 3 * CH)
                return 0

            lax.fori_loop(0, 2, project, 0)
            work.copy(proj, proj_out)
            yield 4.0

            def mix(run, _):
                for at in range(0, RUN, 64):
                    size = 64 if at + 64 < RUN else 56
                    rows = proj[run, at : at + size]
                    ext[run, 8 + at : 8 + at + size] = rows[:, :CH] * rows[:, 2 * CH :]
                return 0

            lax.fori_loop(0, RING, mix, 0)
            yield 0.7
            for copy in sent:
                yield copy
            place_halo(ext, near_out, far_out)

            def convolve(run, _):
                for at in range(0, RUN, 64):
                    for lane in range(2):
                        mixed, one, two = lags(ext, starts, run, at, lane)
                        tap = taps_out[lane]
                        total = tap[2:3] * mixed + tap[1:2] * one + tap[0:1] * two
                        gate = proj[run, at : at + 64, CH + lane * HALF : CH + (lane + 1) * HALF]
                        gated[run, at : at + 64, lane * HALF : (lane + 1) * HALF] = (gate * total).astype(BF16)
                return 0

            lax.fori_loop(0, RING, convolve, 0)
            yield 1.5
            yield "mix_all0"
            yield "mix_all1"
            work.copy(weights.at[0:3], in_out)
            work.copy(weights.at[3:4], mix_out)
            for number, at in enumerate(ring_places(x)):
                out = dot_nn(gated[at], weights[3].reshape(CH, WIDTH))
                parts[at] = out.astype(BF16).reshape(2, SHARD, WIDTH)
                work.set("out" + str(number))
                yield 0.6
            yield "out_done"

            def close(at):
                total = parts[x, k, at].astype(F32) + box[x, at].astype(F32)
                total = total + (land[0, at].astype(F32) + land[1, at].astype(F32))
                rows = tokens[at] + total
                scale = lax.rsqrt(jnp.mean(rows * rows, axis=1, keepdims=True) + NORM_EPS)
                residual[at] = rows
                ffn_in[at] = (rows * scale * gains[1:2]).astype(BF16)

            strips(SHARD, 16, close)
            yield 1.0
            work.set("ffn_in_go")

        def order():
            yield "normed_far"
            work.set("cot_go")

        def follow(half):
            names = ("in", "mix", "gate", "up", "down")
            for name, after in zip(names[:-1], names[1:]):
                yield name + PACE + str(half)
                work.set(after + "_go" + str(half))

        work.add(opening(), 1)
        work.add(gather_x(work, normed.at[x, k], normed, "normed"))
        for half in (0, 1):
            work.add(gather_yz(work, mixer.at[0:3], w_in, half, "in"))
        for half in (0, 1):
            work.add(gather_yz(work, mixer.at[3:4], w_out, half, "mix"))
        for number, name in enumerate(("gate", "up", "down")):
            for half in (0, 1):
                mat = pl.ds(number, 1)
                work.add(gather_yz(work, ffn.at[mat], ffn_out.at[mat], half, name))
        work.add(scatter_x(work, parts, box, hop, land, "out"))
        work.add(gather_x(work, ffn_in, ffn_in_out, "ffn_in", copy=True))
        work.add(gather_x(work, cot, cot_out, "cot", copy=True, hold="out_sent"), 0)
        work.add(order())
        work.add(follow(0))
        work.add(follow(1))
        work.add(compute(), 1)

    gathered = bf(RING, 2, SHARD, WIDTH)
    return call(
        "forward_mixer",
        0,
        body,
        [
            (tokens, VMEM), (cotangent, VMEM), (starts, SMEM), (mixer, VMEM), (ffn, VMEM), (gains, VMEM), (taps, VMEM),
        ],
        [
            (gathered, ANY), (gathered, ANY), (bf(3, 2, HALF, WIDTH), ANY), (bf(1, 2, HALF, WIDTH), ANY),
            (bf(3, 2, HID, WIDTH), ANY), (fl(RING, RUN, 3 * CH), ANY), (fl(RING, 8, CH), VMEM), (fl(8, CH), VMEM),
            (fl(2, 8, HALF), VMEM), (fl(SHARD, WIDTH), VMEM), (gathered, ANY),
        ],
        [
            pltpu.VMEM((RING, 2, SHARD, WIDTH), BF16),
            pltpu.VMEM((4, 2, HALF, WIDTH), BF16),
            pltpu.VMEM((RING, RUN, 3 * CH), F32),
            pltpu.VMEM((RING, RUN + 8, CH), F32),
            pltpu.VMEM((RING, RUN, CH), BF16),
            pltpu.VMEM((RING, 2, SHARD, WIDTH), BF16),
            pltpu.VMEM((RING, SHARD, WIDTH), BF16),
            pltpu.VMEM((2, SHARD // 2, WIDTH), BF16),
            pltpu.VMEM((2, SHARD, WIDTH), BF16),
            pltpu.VMEM((SHARD, WIDTH), BF16),
            pltpu.VMEM((SHARD, WIDTH), BF16),
        ],
        420,
        24,
        X_WAYS + YZ_WAYS + (("z", 2), ("row", 1)),
        int(5e9),
    )


def feed_forward(ffn_in, cot, ffn, residual, cotangent, gains):
    def body(
        work, ffn_in, cot, ffn, residual, cotangent, gains,
        output, grad_residual, grad_out, ffn_grad, gain_part,
        fa, ca, w, gate, up, hid, gg, gu, gh, grad_low,
        parts_a, box_a, hop_a, land_a, parts_b, box_b, hop_b, land_b, boxes,
    ):
        x, k = work.me["x"], work.me["k"]
        units = 2 * HID

        def mat(number):
            return w[number].reshape(units, WIDTH)

        def weight_grad(number, left, right):
            def columns(step, _):
                at = pl.ds(pl.multiple_of(step * 512, 512), 512)
                rows = right[:, :, :, at].reshape(RING * RUN, 512)
                grad = dot_tn(left[...].reshape(RING * RUN, units), rows)
                w[number, :, :, at] = grad.astype(BF16).reshape(2, HID, 512)
                return 0

            lax.fori_loop(0, WIDTH // 512, columns, 0)

        def compute():
            loads = [work.copy(ffn.at[0], w.at[0]), work.copy(ffn_in.at[0:2], fa.at[0:2])]
            loads += [work.copy(ffn.at[1], w.at[1]), work.copy(ffn_in.at[2:4], fa.at[2:4])]
            loads += [work.copy(ffn.at[2], w.at[2]), work.copy(cot, ca)]

            def activate(pair):
                def one(at):
                    for run in (2 * pair, 2 * pair + 1):
                        value = gate[run, at]
                        active = value * jax.nn.sigmoid(value)
                        hid[run, at] = (active * up[run, at]).astype(BF16)

                strips(RUN, 16, one)

            yield loads[0]
            for pair in (0, 1):
                two = pl.ds(2 * pair, 2)
                yield loads[1 if pair == 0 else 3]
                gate[two] = dot_nt(fa[two].reshape(2 * RUN, WIDTH), mat(0)).reshape(2, RUN, units)
                yield 2.0
                if pair == 0:
                    yield loads[2]
                up[two] = dot_nt(fa[two].reshape(2 * RUN, WIDTH), mat(1)).reshape(2, RUN, units)
                yield 2.0
                activate(pair)
                yield 1.2
            yield loads[4]
            for number, at in enumerate(ring_places(x)):
                parts_a[at] = dot_nn(hid[at], mat(2)).astype(BF16).reshape(2, SHARD, WIDTH)
                work.set("down" + str(number))
                yield 1.1
            yield loads[5]
            for pair in (0, 1):
                gh[...] = dot_nt(ca[pl.ds(2 * pair, 2)].reshape(2 * RUN, WIDTH), mat(2)).reshape(2, RUN, units)
                yield 2.0

                def one(at):
                    for here in (0, 1):
                        run = 2 * pair + here
                        value, grad = gate[run, at], gh[here, at]
                        sig = jax.nn.sigmoid(value)
                        gg[run, at] = (grad * up[run, at] * sig * (1.0 + value * (1.0 - sig))).astype(BF16)
                        gu[run, at] = (grad * (value * sig)).astype(BF16)

                strips(RUN, 16, one)
                yield 1.5
            weight_grad(2, hid, ca)
            for half in (0, 1):
                work.set("dwd_go" + str(half))
            yield 4.0
            for number, at in enumerate(ring_places(x)):
                grad = dot_nn(gg[at], mat(0)) + dot_nn(gu[at], mat(1))
                parts_b[at] = grad.astype(BF16).reshape(2, SHARD, WIDTH)
                work.set("gffn" + str(number))
                yield 2.2
            weight_grad(0, gg, fa)
            for half in (0, 1):
                work.set("dwg_go" + str(half))
            yield 4.0
            weight_grad(1, gu, fa)
            for half in (0, 1):
                work.set("dwu_go" + str(half))
            yield 4.0

        def close_down():
            yield "down_done"

            def one(at):
                total = parts_a[x, k, at].astype(F32) + box_a[x, at].astype(F32)
                total = total + (land_a[0, at].astype(F32) + land_a[1, at].astype(F32))
                output[at] = residual[at] + total

            strips(SHARD, 16, one)
            yield 0.4

        def close_grad():
            yield "gffn_done"
            gain_part[...] = jnp.zeros_like(gain_part)

            def one(at):
                grad = parts_b[x, k, at].astype(F32) + box_b[x, at].astype(F32)
                grad = grad + (land_b[0, at].astype(F32) + land_b[1, at].astype(F32))
                rows = residual[at]
                scale = lax.rsqrt(jnp.mean(rows * rows, axis=1, keepdims=True) + NORM_EPS)
                normal = rows * scale
                gain = grad * normal
                gain_part[...] += gain[:8] + gain[8:]
                scaled = grad * gains[1:2]
                back = scale * (scaled - normal * jnp.mean(scaled * normal, axis=1, keepdims=True))
                total = cotangent[at] + back
                grad_residual[at] = total
                grad_low[at] = total.astype(BF16)

            strips(SHARD, 16, one)
            work.set("grad_go")
            yield 1.5

        work.add(scatter_x(work, parts_a, box_a, hop_a, land_a, "down"))
        work.add(scatter_x(work, parts_b, box_b, hop_b, land_b, "gffn"))
        work.add(gather_x(work, grad_low, grad_out, "grad", copy=True))
        for number, name in ((2, "dwd"), (0, "dwg"), (1, "dwu")):
            here = pl.ds(number, 1)
            for half in (0, 1):
                work.add(
                    scatter_yz(work, w.at[here], boxes.at[2 * number + half], ffn_grad.at[here], half, name)
                )
        work.add(compute(), 2)
        work.add(close_grad(), 1)
        work.add(close_down(), 2)

    gathered = bf(RING, 2, SHARD, WIDTH)
    units = 2 * HID
    group = [
        pltpu.VMEM((RING, 2, SHARD, WIDTH), BF16),
        pltpu.VMEM((RING, SHARD, WIDTH), BF16),
        pltpu.VMEM((2, SHARD // 2, WIDTH), BF16),
        pltpu.VMEM((2, SHARD, WIDTH), BF16),
    ]
    return call(
        "feed_forward",
        1,
        body,
        [(ffn_in, ANY), (cot, ANY), (ffn, ANY), (residual, VMEM), (cotangent, VMEM), (gains, VMEM)],
        [
            (fl(SHARD, WIDTH), VMEM), (fl(SHARD, WIDTH), VMEM), (gathered, ANY), (fl(3, HID, CH), VMEM),
            (fl(8, WIDTH), VMEM),
        ],
        [
            pltpu.VMEM((RING, 2, SHARD, WIDTH), BF16),
            pltpu.VMEM((RING, 2, SHARD, WIDTH), BF16),
            pltpu.VMEM((3, 2, HID, WIDTH), BF16),
            pltpu.VMEM((RING, RUN, units), F32),
            pltpu.VMEM((RING, RUN, units), F32),
            pltpu.VMEM((RING, RUN, units), BF16),
            pltpu.VMEM((RING, RUN, units), BF16),
            pltpu.VMEM((RING, RUN, units), BF16),
            pltpu.VMEM((2, RUN, units), F32),
            pltpu.VMEM((SHARD, WIDTH), BF16),
            *group,
            *group,
            pltpu.VMEM((6, 15, 1, HID, HALF), BF16),
        ],
        240,
        12,
        X_WAYS + YZ_WAYS,
        int(27e9),
    )


def backward_mixer(
    grad_low, normed, w_in, w_out, proj, near, far, taps, starts, tokens, grad_residual, gains, gain_two
):
    def body(
        work, grad_low, normed, w_in, w_out, proj_in, near, far, taps, starts, tokens, grad_residual, gains, gain_two,
        input_grad, mixer_grad, small_out,
        ga, na, w, proj, ext, ahead, conv, gated, gp, near_next, far_next, tap_sum, gain_sum, small,
        parts, box, hop, land, box_mix, box_in, box_small,
    ):
        x, k = work.me["x"], work.me["k"]
        row, col = lax.axis_index("row"), lax.axis_index("col")
        late = (col // 2) % 2 == 1

        def mat_in():
            return w[0:3].reshape(3 * CH, WIDTH)

        def compute():
            loads = [work.copy(proj_in, proj), work.copy(w_out, w.at[3:4]), work.copy(grad_low, ga)]
            loads += [work.copy(w_in, w.at[0:3]), work.copy(normed, na)]
            yield loads[0]

            def mix(run, _):
                for at in range(0, RUN, 64):
                    rows = proj[run, at : at + 64]
                    ext[run, 8 + at : 8 + at + 64] = rows[:, :CH] * rows[:, 2 * CH :]
                return 0

            lax.fori_loop(0, RING, mix, 0)
            place_halo(ext, near, far)

            def convolve(run, _):
                for at in range(0, RUN, 64):
                    for lane in range(2):
                        lanes = slice(lane * HALF, (lane + 1) * HALF)
                        mixed, one, two = lags(ext, starts, run, at, lane)
                        tap = taps[lane]
                        total = tap[2:3] * mixed + tap[1:2] * one + tap[0:1] * two
                        gate = proj[run, at : at + 64, CH + lane * HALF : CH + (lane + 1) * HALF]
                        conv[run, at : at + 64, lanes] = total
                        gated[run, at : at + 64, lanes] = (gate * total).astype(BF16)
                return 0

            lax.fori_loop(0, RING, convolve, 0)
            yield 2.2
            yield loads[1]
            yield loads[2]

            def gate_back(pair, _):
                two = pl.ds(2 * pair, 2)
                grad = dot_nt(ga[two].reshape(2 * RUN, WIDTH), w[3].reshape(CH, WIDTH)).reshape(2, RUN, CH)
                ahead[two, 0:RUN] = grad * proj[two, :, CH : 2 * CH]
                gp[two, :, CH : 2 * CH] = (grad * conv[two]).astype(BF16)
                return 0

            lax.fori_loop(0, 2, gate_back, 0)
            sent = [
                work.send(ahead.at[:, 0:8], near_next, ("z", 2)),
                work.send(ahead.at[0, 0:8], far_next, ("row", -1)),
            ]
            yield 2.5

            def out_grad(step, _):
                at = pl.ds(pl.multiple_of(step * 512, 512), 512)
                rows = ga[:, :, :, at].reshape(RING * RUN, 512)
                grad = dot_tn(gated[...].reshape(RING * RUN, CH), rows)
                w[3, :, :, at] = grad.astype(BF16).reshape(2, HALF, 512)
                return 0

            lax.fori_loop(0, WIDTH // 512, out_grad, 0)
            for half in (0, 1):
                work.set("mix_go" + str(half))
            yield 1.7
            for copy in sent:
                yield copy
            last = jnp.where(row < ROWS - 1, far_next[...], 0.0)
            for run in range(RING):
                after = last if run == RING - 1 else near_next[run + 1]
                ahead[run, RUN : RUN + 8] = jnp.where(late, after, near_next[run])
            tap_sum[...] = jnp.zeros_like(tap_sum)

            def unmix(run, _):
                for at in range(0, RUN, 64):
                    for lane in range(2):
                        lanes = slice(lane * HALF, (lane + 1) * HALF)
                        rows = slice(at, at + 64)
                        first = run_start(run, RUN) + at
                        one, _two = keeps(starts, first + 1, (64, HALF))
                        _one, two = keeps(starts, first + 2, (64, HALF))
                        tap = taps[lane]
                        grad = ahead[run, rows, lanes]
                        mixed, lag_one, lag_two = lags(ext, starts, run, at, lane)
                        for number, value in enumerate((lag_two, lag_one, mixed)):
                            tap_sum[number, :, lanes] += jnp.sum((grad * value).reshape(8, 8, HALF), axis=0)
                        total = tap[2:3] * grad + tap[1:2] * (one * ahead[run, at + 1 : at + 65, lanes])
                        total = total + tap[0:1] * (two * ahead[run, at + 2 : at + 66, lanes])
                        conv_in = proj[run, rows, 2 * CH + lane * HALF : 2 * CH + (lane + 1) * HALF]
                        gate = proj[run, rows, lanes]
                        gp[run, rows, lanes] = (total * conv_in).astype(BF16)
                        gp[run, rows, 2 * CH + lane * HALF : 2 * CH + (lane + 1) * HALF] = (total * gate).astype(BF16)
                return 0

            lax.fori_loop(0, RING, unmix, 0)
            yield 3.0
            yield loads[3]
            for number, at in enumerate(ring_places(x)):
                parts[at] = dot_nn(gp[at], mat_in()).astype(BF16).reshape(2, SHARD, WIDTH)
                work.set("normed" + str(number))
                yield 1.1
            yield loads[4]

            def in_grad(step, _):
                at = pl.ds(pl.multiple_of(step * 512, 512), 512)
                rows = na[:, :, :, at].reshape(RING * RUN, 512)
                grad = dot_tn(gp[...].reshape(RING * RUN, 3 * CH), rows)
                old = w[0:3, :, :, at].reshape(3 * CH, 512).astype(F32)
                gain_sum[:, at] = jnp.sum((grad * old).reshape(3 * CH // 8, 8, 512), axis=0)
                w[0:3, :, :, at] = grad.astype(BF16).reshape(3, 2, HALF, 512)
                return 0

            lax.fori_loop(0, WIDTH // 512, in_grad, 0)
            for half in (0, 1):
                work.set("in_go" + str(half))
            small[...] = jnp.zeros_like(small)
            small[0:1] = jnp.sum(gain_sum[...], axis=0, keepdims=True) / gains[0:1]
            small[1:2] = jnp.sum(gain_two[...], axis=0, keepdims=True)
            mine = pl.ds(pl.multiple_of((x * 2 + k) * CH, CH), CH)
            for number in range(3):
                small[2 + number : 3 + number, mine] = jnp.sum(tap_sum[number], axis=0, keepdims=True)
            work.set("small_go")
            yield 4.5

        def close():
            yield "normed_done"

            def one(at):
                grad = parts[x, k, at].astype(F32) + box[x, at].astype(F32)
                grad = grad + (land[0, at].astype(F32) + land[1, at].astype(F32))
                rows = tokens[at]
                scale = lax.rsqrt(jnp.mean(rows * rows, axis=1, keepdims=True) + NORM_EPS)
                normal = rows * scale
                scaled = grad * gains[0:1]
                back = scale * (scaled - normal * jnp.mean(scaled * normal, axis=1, keepdims=True))
                input_grad[at] = grad_residual[at] + back

            strips(SHARD, 16, one)
            yield 1.2

        work.add(scatter_x(work, parts, box, hop, land, "normed"))
        for half in (0, 1):
            work.add(scatter_yz(work, w.at[3:4], box_mix.at[half], mixer_grad.at[3:4], half, "mix"))
        for half in (0, 1):
            work.add(scatter_yz(work, w.at[0:3], box_in.at[half], mixer_grad.at[0:3], half, "in"))
        work.add(sum_all(work, small, box_small, small_out, "small"))
        work.add(compute(), 1)
        work.add(close(), 1)

    return call(
        "backward_mixer",
        2,
        body,
        [
            (grad_low, ANY), (normed, ANY), (w_in, ANY), (w_out, ANY), (proj, ANY), (near, VMEM), (far, VMEM),
            (taps, VMEM), (starts, SMEM), (tokens, VMEM), (grad_residual, VMEM), (gains, VMEM), (gain_two, VMEM),
        ],
        [(fl(SHARD, WIDTH), VMEM), (fl(4, HALF, CH), VMEM), (fl(8, WIDTH), VMEM)],
        [
            pltpu.VMEM((RING, 2, SHARD, WIDTH), BF16),
            pltpu.VMEM((RING, 2, SHARD, WIDTH), BF16),
            pltpu.VMEM((4, 2, HALF, WIDTH), BF16),
            pltpu.VMEM((RING, RUN, 3 * CH), F32),
            pltpu.VMEM((RING, RUN + 8, CH), F32),
            pltpu.VMEM((RING, RUN + 8, CH), F32),
            pltpu.VMEM((RING, RUN, CH), F32),
            pltpu.VMEM((RING, RUN, CH), BF16),
            pltpu.VMEM((RING, RUN, 3 * CH), BF16),
            pltpu.VMEM((RING, 8, CH), F32),
            pltpu.VMEM((8, CH), F32),
            pltpu.VMEM((3, 8, CH), F32),
            pltpu.VMEM((8, WIDTH), F32),
            pltpu.VMEM((8, WIDTH), F32),
            pltpu.VMEM((RING, 2, SHARD, WIDTH), BF16),
            pltpu.VMEM((RING, SHARD, WIDTH), BF16),
            pltpu.VMEM((2, SHARD // 2, WIDTH), BF16),
            pltpu.VMEM((2, SHARD, WIDTH), BF16),
            pltpu.VMEM((2, 15, 1, HALF, HALF), BF16),
            pltpu.VMEM((2, 15, 3, HALF, HALF), BF16),
            pltpu.VMEM((4, RING, 8, WIDTH), F32),
        ],
        160,
        8,
        X_WAYS + YZ_WAYS + (("z", 2), ("y", 2), ("x", 2), ("row", -1)),
        int(9e9),
    )


def adam_update(weight, gradient, first, second, step_rate, decay_rate):
    first_new = BETA_ONE * first + (1.0 - BETA_ONE) * gradient
    second_new = BETA_TWO * second + (1.0 - BETA_TWO) * gradient * gradient
    first_hat = first_new / (1.0 - BETA_ONE**STEP)
    second_hat = second_new / (1.0 - BETA_TWO**STEP)
    weight_new = weight - step_rate * (
        first_hat / (jnp.sqrt(second_hat) + ADAM_EPS) + decay_rate * weight
    )
    return (weight_new, first_new, second_new)


def body(
    tokens,
    cotangent,
    doc_starts,
    mixer_w,
    ffn_w,
    gains,
    taps,
    mixer_m,
    mixer_v,
    ffn_m,
    ffn_v,
    gain_m,
    gain_v,
    tap_m,
    tap_v,
):
    col = lax.axis_index("col")
    mixer_low = jnp.swapaxes(mixer_w.astype(BF16), 1, 2)
    ffn_low = jnp.swapaxes(ffn_w.astype(BF16), 1, 2)
    taps_pad = jnp.concatenate([taps, jnp.zeros((5, HALF), F32)], axis=0)
    normed, cot, w_in, w_out, ffn, proj, near, far, taps_two, residual, ffn_in = forward_mixer(
        tokens, cotangent, doc_starts, mixer_low, ffn_low, gains, taps_pad
    )
    output, grad_residual, grad_low, ffn_grad, gain_two = feed_forward(
        ffn_in, cot, ffn, residual, cotangent, gains
    )
    input_grad, mixer_grad, total = backward_mixer(
        grad_low, normed, w_in, w_out, proj, near, far, taps_two, doc_starts, tokens, grad_residual, gains, gain_two
    )
    mixer_grad = jnp.swapaxes(mixer_grad, 1, 2)
    ffn_grad = jnp.swapaxes(ffn_grad, 1, 2)
    gain_grad = total[:2]
    first = ((col // 4) * 2 + col % 2) * CH + (col // 2) % 2 * HALF
    tap_grad = lax.dynamic_slice_in_dim(total[2:5], first, HALF, 1)

    mixer_new, mixer_m_new, mixer_v_new = adam_update(
        mixer_w, mixer_grad, mixer_m, mixer_v, MATRIX_RATE, MATRIX_DECAY
    )
    ffn_new, ffn_m_new, ffn_v_new = adam_update(
        ffn_w, ffn_grad, ffn_m, ffn_v, MATRIX_RATE, MATRIX_DECAY
    )
    gain_new, gain_m_new, gain_v_new = adam_update(
        gains, gain_grad, gain_m, gain_v, SMALL_RATE, 0.0
    )
    tap_new, tap_m_new, tap_v_new = adam_update(taps, tap_grad, tap_m, tap_v, SMALL_RATE, 0.0)
    return (
        output,
        input_grad,
        mixer_grad,
        mixer_new,
        mixer_m_new,
        mixer_v_new,
        ffn_grad,
        ffn_new,
        ffn_m_new,
        ffn_v_new,
        gain_grad,
        gain_new,
        gain_m_new,
        gain_v_new,
        tap_grad,
        tap_new,
        tap_m_new,
        tap_v_new,
    )


def solution(mesh):
    placed = (
        P(("row", "col"), None),
        P(("row", "col"), None),
        P(),
        P(None, "row", "col"),
        P(None, "row", "col"),
        P(),
        P(None, "col"),
        P(None, "row", "col"),
        P(None, "row", "col"),
        P(None, "row", "col"),
        P(None, "row", "col"),
        P(),
        P(),
        P(None, "col"),
        P(None, "col"),
    )
    return jax.shard_map(
        body,
        mesh=mesh,
        in_specs=placed,
        out_specs=(
            P(("row", "col"), None),
            P(("row", "col"), None),
            P(None, "row", "col"),
            P(None, "row", "col"),
            P(None, "row", "col"),
            P(None, "row", "col"),
            P(None, "row", "col"),
            P(None, "row", "col"),
            P(None, "row", "col"),
            P(None, "row", "col"),
            P(),
            P(),
            P(),
            P(),
            P(None, "col"),
            P(None, "col"),
            P(None, "col"),
            P(None, "col"),
        ),
        check_vma=False,
    )
```

time: 1240 us -> 282 us (0.23)
  waiting for transfers between devices: 1000 us -> 0 us
  Pallas kernels: 0 us -> 253 us
  matrix products: 97 us -> 0 us
  blocking collectives: 65.9 us -> 0 us
  other arithmetic: 34.9 us -> 9.94 us
  between operations: 14.9 us -> 0.99 us
    reduce_scatter x6 -> x0, waiting for transfers between devices: 591 us -> none  [the longest x1 145 us: body(): lax.psum_scatter(partial_out, 'col', scatter_dimension=0, tiled=True)]
    all_gather x6 -> x0, waiting for transfers between devices: 408 us -> none  [the longest x1 87.4 us: body(): lax.all_gather(ffn_w.astype(jnp.bfloat16), 'row', axis=1, tiled=True)]
    pallas_call x0 -> x3, Pallas kernels: none -> 253 us  [call(): pl.pallas_call(kernel, out_shape=[shape for shape, _ in outs], in_specs=[...]
    dot_general x12 -> x0, matrix products: 97 us -> none  [the longest x2 21.7 us: trans_dot(): lax.dot_general(left, right, (((1,), (1,)), ((), ())), preferred_element_...]
    psum x1 -> x0, blocking collectives: 65.9 us -> none  [body(): lax.psum((jnp.stack([gain_one_part, gain_two_part]), tap_placed), ('row',...]
    convert_element_type x7 -> x0, other arithmetic: 12.9 us -> none  [the longest x1 3.53 us: body(): grad_residual.astype(jnp.bfloat16)]
  transfers between devices with their start and end apart: 14 -> 0, of which waited for: 14 -> 0; matrix products, arithmetic and copies ran while one was open for 8% -> 0% of each run, Pallas kernels for 0% -> 0%
where the time goes in v1:
time: 282 us; the launch traced here: 276 us
  Pallas kernels  253 us (90%)
  local copies, waits for them, and re-layouts  12.4 us (4%)
  other arithmetic  9.94 us (4%)
    pallas_call x3, Pallas kernels, call(): pl.pallas_call(kernel, out_shape=[shape for shape, _ in outs], in_specs=[...  253 us
    unnamed x38, local copies, waits for them, and re-layouts  10.9 us
    sub x4, other arithmetic, adam_update(): weight - step_rate * (first_hat / (jnp.sqrt(second_hat) + ADAM_EPS) + dec...  8.36 us

profile of v1, /device:TPU:1, one launch (start us, length us, event | category | flops | bytes accessed | tf_op | source)
XLA Modules:
  0.0 276.5 jit_solution(4846096843824861314)
XLA Ops:
  0.7 0.0 copy-start
  0.7 1.3 copy.33
  2.0 0.0 copy-start.11
  2.0 0.7 convert_bitcast_fusion.1.refs_3_
  2.7 0.9 convert_bitcast_fusion.refs_4_
  3.6 0.6 concatenate.3.refs_6_
  4.2 104.5 %forward_mixer.1 = (bf16[4,2,128,2048]{3,2,1,0:T(8,128)(2,1)}, bf16[4,2,128,2048]{3,2,1,0:T(8,128)(2,1)}, bf16[3,2,128,2048]{3,2,1,0:T(8,128)(2,1)}, bf16[1,2,12...) custom-call(f32[128,2048]{1,0:T(8,128)} %refs_9_.1, ...), custom_call_target="tpu_custom_call" | custom-call | flops 5000000000 | bytes 41943040 | tf_op jit(solution)/shard_map/forward_mixer/pallas_call | solution.py:452
  108.7 87.7 %feed_forward.1 = (f32[128,2048]{1,0:T(8,128)}, f32[128,2048]{1,0:T(8,128)}, bf16[4,2,128,2048]{3,2,1,0:T(8,128)(2,1)}, f32[3,352,256]{2,1,0:T(8,128)}, f32[8,2048]{1,0:T(8,128)}) custom-call(bf16[4,2,128,2048]{3,2,1,0:T(8,128)(2,1)} %get-tuple-element.37.refs_0_, bf16[4,2,128,2048]{3,2,1,0:T(8,128)(2,1)} %get-tuple-element.38.refs_1_, ...), custom_call_target="tpu_custom_call" | custom-call | flops 27000000512 | bytes 41943040 | tf_op jit(solution)/shard_map/feed_forward/pallas_call | solution.py:452
  196.5 0.0 copy-start.12
  196.5 0.0 copy-start.13
  196.5 0.0 copy-start.6
  196.5 60.9 %backward_mixer.1 = (f32[128,2048]{1,0:T(8,128)}, f32[4,128,256]{2,1,0:T(8,128)}, f32[8,2048]{1,0:T(8,128)}) custom-call(bf16[4,2,128,2048]{3,2,1,0:T(8,128)(2,1)} %get-tuple-element.42.refs_0_, bf16[4,2,128,2048]{3,2,1,0:T(8,128)(2,1)} %get-tuple-element.43.refs_1_, bf16[3,2,128,2048]{3,2,1,0:T(8,128)(2,1)} %get-tuple-element.44.refs_2_, ...), custom_call_target="tpu_custom_call" | custom-call | flops 8999999488 | bytes 41943040 | tf_op jit(solution)/shard_map/backward_mixer/pallas_call | solution.py:452
  257.4 0.0 copy-start.7
  257.4 0.9 slice.7
  258.3 0.6 multiply_subtract_fusion.3
  258.9 1.0 copy.34
  259.9 1.0 copy.35
  260.9 0.0 copy-done.2
  260.9 2.4 multiply_subtract_fusion.1
  263.3 1.0 copy.39
  264.3 1.0 copy.40
  265.3 0.0 copy-start.1
  265.3 1.0 copy.41
  266.3 1.0 copy.38
  267.3 0.0 copy-done.8
  267.3 0.0 copy-done.10
  267.3 1.5 multiply_subtract_fusion.2
  268.9 3.9 %multiply_subtract_fusion = (f32[3,256,352]{1,2,0:T(8,128)}, f32[3,256,352]{1,2,0:T(8,128)}, f32[3,256,352]{1,2,0:T(8,128)}) fusion(f32[3,256,352]{1,2,0:T(8,128)S(1)} %copy-done, f32[3,256,352]{1,2,0:T(8,128)} %param.24, f32[3,256,352]{1,2,0:T(8,128)} %param.25, f32[3,352,256]{2,1,0:T(8,128)S(1)} %copy-done.1), kind=kLoop, calls=%fused_computation.2 | loop fusion | flops 4055040 | bytes 7569408 | tf_op jit(solution)/shard_map/sub | solution.py:1069
  272.7 1.0 copy.45
  273.7 0.6 copy-done.5
  274.3 1.0 copy.46
  275.3 1.0 copy.47
  (17 shorter events, 0.0 us)
Async XLA Ops:
  0.7 2.1 copy-start
  2.0 1.6 copy-start.11
  196.5 61.9 %copy-start.12 = (f32[3,128]{1,0:T(4,128)S(1)}, f32[3,128]{1,0:T(4,128)}, u32[]{:S(2)}) copy-start(f32[3,128]{1,0:T(4,128)} %param.28) | copy-start | bytes 4612
  196.5 61.9 %copy-start.13 = (f32[3,128]{1,0:T(4,128)S(1)}, f32[3,128]{1,0:T(4,128)}, u32[]{:S(2)}) copy-start(f32[3,128]{1,0:T(4,128)} %param.29) | copy-start | bytes 4612
  196.5 62.5 %copy-start.6 = (f32[4,256,128]{2,1,0:T(8,128)S(1)}, f32[4,256,128]{2,1,0:T(8,128)}, u32[]{:S(2)}) copy-start(f32[4,256,128]{2,1,0:T(8,128)} %param.22) | copy-start | bytes 1572868
  257.4 2.6 copy-start.7
  258.3 2.7 copy-start.2
  263.3 2.0 copy-start.3
  265.3 2.0 copy-start.8
  265.3 2.0 copy-start.9
  265.3 2.0 copy-start.10
  265.3 3.5 %copy-start.1 = (f32[3,352,256]{2,1,0:T(8,128)S(1)}, f32[3,352,256]{2,1,0:T(8,128)}, u32[]{:S(2)}) copy-start(f32[3,352,256]{2,1,0:T(8,128)} %get-tuple-element.54) | copy-start | bytes 3244036
  268.9 3.9 %copy-start.4 = (f32[128,2048]{1,0:T(8,128)S(1)}, f32[128,2048]{1,0:T(8,128)}, u32[]{:S(2)}) copy-start(f32[128,2048]{1,0:T(8,128)} %get-tuple-element.106) | copy-start | bytes 3145732
  272.7 1.6 copy-start.5
